TPU v7x, 256 devices: a whole 4x4x8 slice. The times are simulated.
256 devices in a mesh: cuts: 4 (over x), gx: 8 (over z_lo, core), gy: 8 (over y, z_hi).
Axes of the slice: x: 4, y: 4, z: 8 (z_hi: 2, z_lo: 4; z = z_hi * 4 + z_lo), core: 2. Of those that a mesh axis runs over, the one named last changes fastest.
Arguments:
- slice_starts: float32 [4, 5, 256, 256, 128], P('cuts', None, 'gx', 'gy'), may hold values from -6 to 6
Outputs:
- new_states: float32 [4, 5, 256, 256, 128], P('cuts', None, 'gx', 'gy')
All inputs are finite; a program needn't handle non-finite values.
Results may differ from a plain program's by a relative error of at most 0.00011.
Values sent between devices are 32-bit elements; how exact they have to be, the bound alone decides.
A program may use at most 64 MiB of HBM per device.

v0:
```python
import jax
import jax.numpy as jnp
from jax import lax
from jax.experimental import pallas as pl
from jax.experimental.pallas import tpu as pltpu
from jax.sharding import PartitionSpec as P

TIME_STEP = 0.1
VISCOSITY = 0.2
MESH = pl.DeviceIdType.MESH
NB = 32
NC = 16
X0 = 8
FIELDS = range(5)


def stencil(C, E, W, N, S, A, B, top, bottom, spacing, step):
    g = step / (2.0 * spacing)
    k = VISCOSITY * step / (spacing * spacing)
    centre = 1.0 - 6.0 * k
    zero = jnp.zeros_like(C[0])
    gu, gv, gw = g * C[0], g * C[1], g * C[2]
    ce, cw = k - gu, k + gu
    cn, cs = k - gv, k + gv
    ca = jnp.where(top, zero, k - gw)
    cb = jnp.where(bottom, zero, k + gw)
    out = []
    for q in range(4):
        out.append(
            (centre * C[q] + ce * E[q] + cw * W[q])
            + (cn * N[q] + cs * S[q])
            + (ca * A[q] + cb * B[q])
        )
    rise_p = jnp.where(top, zero, A[4]) - jnp.where(bottom, zero, B[4])
    rise_w = jnp.where(top, zero, A[2]) - jnp.where(bottom, zero, B[2])
    out[0] = out[0] - g * (E[4] - W[4])
    out[1] = out[1] - g * (N[4] - S[4])
    out[2] = out[2] + (step * C[3] - g * rise_p)
    out[3] = out[3] + step * C[2]
    out.append(C[4] - g * ((E[0] - W[0]) + (N[1] - S[1]) + rise_w))
    return out


def lanes():
    return lax.broadcasted_iota(jnp.int32, (8, 128), 1)


def sublanes():
    return lax.broadcasted_iota(jnp.int32, (8, 128), 0)


def lane_up(v, n=1):
    return pltpu.roll(v, 128 - n, 1)


def lane_down(v, n=1):
    return pltpu.roll(v, n, 1)


def fine_tile(src, dst, ys, yd, rs, rd, top, bottom):
    C = [src[f, ys, pl.ds(rs, 8), :] for f in FIELDS]
    E = [src[f, ys, pl.ds(rs + 1, 8), :] for f in FIELDS]
    W = [src[f, ys, pl.ds(rs - 1, 8), :] for f in FIELDS]
    N = [src[f, ys + 1, pl.ds(rs, 8), :] for f in FIELDS]
    S = [src[f, ys - 1, pl.ds(rs, 8), :] for f in FIELDS]
    A = [lane_up(c) for c in C]
    B = [lane_down(c) for c in C]
    out = stencil(C, E, W, N, S, A, B, top, bottom, 1.0, TIME_STEP)
    for f in FIELDS:
        dst[f, yd, pl.ds(rd, 8), :] = out[f]


def restrict_row(src, y, x0, even):
    out = []
    for f in FIELDS:
        halves = []
        for base in (x0, x0 + 16):
            total = None
            for plane in (y, y + 1):
                for start in (base, base + 1):
                    part = src[f, plane, pl.ds(start, 8, stride=2), :]
                    total = part if total is None else total + part
            halves.append(total)
        low, high = halves
        out.append(0.125 * jnp.where(even, low + lane_up(low), high + lane_down(high)))
    return out


def coarse_row(C, N, S, H, even, sub, top, bottom):
    E, W = [], []
    for f in FIELDS:
        r_w = pltpu.roll(C[f], 1, 0)
        r_e = pltpu.roll(C[f], 7, 0)
        mixed = jnp.where(sub == 0, jnp.where(even, r_w, H[f]), jnp.where(even, H[f], r_e))
        swapped = jnp.where(even, lane_up(mixed), lane_down(mixed))
        W.append(jnp.where(sub == 0, swapped, r_w))
        E.append(jnp.where(sub == 7, swapped, r_e))
    A = [lane_up(c, 2) for c in C]
    B = [lane_down(c, 2) for c in C]
    return stencil(C, E, W, N, S, A, B, top, bottom, 2.0, 2.0 * TIME_STEP)


def kernel(x_ref, o_ref, s0, s1, fine, rs, hs, gr, cin, hin, cout,
           load_sem, out_sem, halo_send, halo_recv, chain_send, chain_recv):
    n = lax.axis_index("cuts")
    gx = lax.axis_index("gx")
    gy = lax.axis_index("gy")

    def at(dn, dx, dy):
        return (lax.rem(n + 4 + dn, 4), lax.rem(gx + 8 + dx, 8), lax.rem(gy + 8 + dy, 8))

    star = [(0, 0), (1, 0), (-1, 0), (0, 1), (0, -1)]
    partners = [(0, dx, dy) for dx in (-1, 0, 1) for dy in (-1, 0, 1) if (dx, dy) != (0, 0)]
    partners += [(dn, dx, dy) for dn in (1, -1) for dx, dy in star]
    barrier = pltpu.get_barrier_semaphore()
    for p in partners:
        pl.semaphore_signal(barrier, inc=1, device_id=at(*p), device_id_type=MESH)

    @pl.loop(0, NB)
    def _(y):
        pltpu.make_async_copy(
            x_ref.at[:, :, y, :], s0.at[:, y + 2, pl.ds(X0, NB), :], load_sem
        ).start()

    pl.semaphore_wait(barrier, len(partners))

    halos = []

    def send(src, dst, where):
        i = len(halos)
        copy = pltpu.make_async_remote_copy(
            src_ref=src, dst_ref=dst, send_sem=halo_send.at[i], recv_sem=halo_recv.at[i],
            device_id=at(*where), device_id_type=MESH,
        )
        copy.start()
        halos.append(copy)

    own = pl.ds(2, NB)
    for step in range(2):
        send(x_ref.at[:, 30 + step, :, :], s0.at[:, own, 6 + step, :], (0, 1, 0))
        send(x_ref.at[:, step, :, :], s0.at[:, own, 40 + step, :], (0, -1, 0))
    for dx, x_from, x_to in ((1, 31, 7), (-1, 0, 40)):
        for dy, y_from, y_to in ((1, 31, 1), (-1, 0, 34)):
            send(x_ref.at[:, x_from, y_from, :], s0.at[:, y_to, x_to, :], (0, dx, dy))
    rows = pl.ds(X0, NB)
    for step in range(2):
        send(x_ref.at[:, :, 30 + step, :], s0.at[:, step, rows, :], (0, 0, 1))
        send(x_ref.at[:, :, step, :], s0.at[:, 34 + step, rows, :], (0, 0, -1))
    gx_halos, gy_halos = halos[:4], halos[4:]

    lane = lanes()
    sub = sublanes()
    even = lane % 2 == 0
    top, bottom = lane == 127, lane == 0
    ctop, cbottom = lane >= 126, lane <= 1

    def first_plane(y, wide):
        starts = (7, 15, 23, 31, 39) if wide else (8, 16, 24, 32)
        for r in starts:
            fine_tile(s0, s1, y + 2, y + 1, r, r, top, bottom)

    def second_plane(y):
        for r in range(0, NB, 8):
            fine_tile(s1, fine, y + 1, y, r + X0, r, top, bottom)

    def put_rs(j):
        out = restrict_row(s0, 2 * j + 2, X0, even)
        for f in FIELDS:
            rs[f, j + 1] = out[f]

    def put_hs(j):
        for f in FIELDS:
            total = None
            for plane in (2 * j + 2, 2 * j + 3):
                west = s0[f, plane, pl.ds(6, 8), :] + s0[f, plane, pl.ds(7, 8), :]
                east = s0[f, plane, pl.ds(33, 8), :] + s0[f, plane, pl.ds(34, 8), :]
                part = jnp.where(sub == 0, west, east)
                total = part if total is None else total + part
            hs[f, j] = 0.125 * (total + jnp.where(even, lane_up(total), lane_down(total)))

    def coarse_of(state, halo, j):
        C = [state[f, j + 1] for f in FIELDS]
        N = [state[f, j + 2] for f in FIELDS]
        S = [state[f, j] for f in FIELDS]
        H = [halo[f, j] for f in FIELDS]
        return coarse_row(C, N, S, H, even, sub, ctop, cbottom)

    def put_gr(j):
        out = coarse_of(rs, hs, j)
        for f in FIELDS:
            gr[f, j] = out[f]

    def put_rf(j):
        out = restrict_row(fine, 2 * j, 0, even)
        for f in FIELDS:
            cout[f, j] = out[f]

    pltpu.make_async_copy(x_ref, s0.at[:, own, rows, :], load_sem).wait()
    for copy in gx_halos:
        copy.wait_recv()

    pl.loop(1, NB - 1)(lambda y: first_plane(y, True))
    pl.loop(2, NB - 2)(second_plane)

    def early_row(j):
        put_rf(j)

    pl.loop(1, NC - 1)(early_row)

    def chain_copies(k, late):
        copies = []
        edge = k + 1
        if late:
            spans = [(0, edge, 3), (NC - edge, edge, 6)]
        else:
            spans = [(edge, NC - 2 * edge, 0)]

        def add(src, dst, where, i):
            copies.append(pltpu.make_async_remote_copy(
                src_ref=src, dst_ref=dst, send_sem=chain_send.at[i], recv_sem=chain_recv.at[i],
                device_id=at(*where), device_id_type=MESH,
            ))

        if late:
            add(cout.at[:, 0], cin.at[:, NC + 1], (1, 0, -1), 9)
            add(cout.at[:, NC - 1], cin.at[:, 0], (1, 0, 1), 10)
        for first, count, i in spans:
            span = pl.ds(first, count)
            add(cout.at[:, span, 7, :], hin.at[:, span, 0, :], (1, 1, 0), i + 1)
            add(cout.at[:, span, 0, :], hin.at[:, span, 7, :], (1, -1, 0), i + 2)
            add(cout.at[:, span], cin.at[:, pl.ds(first + 1, count)], (1, 0, 0), i)
        return copies

    def start_chain(k, late):
        @pl.when(n == k)
        def _():
            for copy in chain_copies(k, late):
                copy.start()

    def wait_chain(k, late):
        @pl.when(n == k + 1)
        def _():
            for copy in chain_copies(k, late):
                copy.wait_recv()

    start_chain(0, False)

    @pl.loop(0, NC)
    def _(j):
        put_rs(j)
        put_hs(j)

    pl.loop(1, NC - 1)(put_gr)

    for copy in gy_halos:
        copy.wait_recv()

    @pl.loop(0, 2)
    def _(side):
        first_plane(side * 33 - 1, False)
        first_plane(side * 31, True)

    @pl.loop(0, 2)
    def _(side):
        second_plane(side * 30)
        second_plane(side * 30 + 1)

    @pl.loop(0, 2)
    def _(side):
        put_rf(side * 15)

    start_chain(0, True)

    @pl.loop(0, 2)
    def _(side):
        put_rs(side * 17 - 1)

    @pl.loop(0, 2)
    def _(side):
        put_gr(side * 15)

    def write_planes(j):
        for y in (2 * j, 2 * j + 1):
            pltpu.make_async_copy(fine.at[:, y], o_ref.at[:, :, y, :], out_sem).start()

    @pl.when(n == 0)
    def _():
        pl.loop(0, NC)(write_planes)

    def chain_row(j):
        out = coarse_of(cin, hin, j)
        for f in FIELDS:
            d = out[f] - gr[f, j]
            cout[f, j] = cout[f, j] + d
            low = jnp.where(even, d, lane_down(d))
            high = jnp.where(even, lane_up(d), d)
            for y in (2 * j, 2 * j + 1):
                for start, part in ((0, low), (1, low), (16, high), (17, high)):
                    span = pl.ds(start, 8, stride=2)
                    fine[f, y, span, :] = fine[f, y, span, :] + part
        write_planes(j)

    for k in range(3):
        wait_chain(k, False)

    @pl.when(n > 0)
    def _():
        pl.loop(n + 1, NC - 1 - n)(chain_row)

    for k in (1, 2):
        start_chain(k, False)

    for k in range(3):
        wait_chain(k, True)

    @pl.when(n > 0)
    def _():
        pl.loop(0, n + 1)(chain_row)
        pl.loop(NC - 1 - n, NC)(chain_row)

    for k in (1, 2):
        start_chain(k, True)

    for copy in halos:
        copy.wait_send()
    for k in range(3):
        @pl.when(n == k)
        def _():
            for late in (False, True):
                for copy in chain_copies(k, late):
                    copy.wait_send()

    pltpu.make_async_copy(fine, o_ref, out_sem).wait()


def body(slice_starts):
    fields = slice_starts[0]
    f32 = jnp.float32
    out = pl.pallas_call(
        kernel,
        out_shape=jax.ShapeDtypeStruct(fields.shape, f32),
        in_specs=[pl.BlockSpec(memory_space=pl.ANY)],
        out_specs=pl.BlockSpec(memory_space=pl.ANY),
        scratch_shapes=[
            pltpu.VMEM((5, 36, 48, 128), f32),
            pltpu.VMEM((5, 34, 48, 128), f32),
            pltpu.VMEM((5, NB, NB, 128), f32),
            pltpu.VMEM((5, NC + 2, 8, 128), f32),
            pltpu.VMEM((5, NC, 8, 128), f32),
            pltpu.VMEM((5, NC, 8, 128), f32),
            pltpu.VMEM((5, NC + 2, 8, 128), f32),
            pltpu.VMEM((5, NC, 8, 128), f32),
            pltpu.VMEM((5, NC, 8, 128), f32),
            pltpu.SemaphoreType.DMA,
            pltpu.SemaphoreType.DMA,
            pltpu.SemaphoreType.DMA((12,)),
            pltpu.SemaphoreType.DMA((12,)),
            pltpu.SemaphoreType.DMA((11,)),
            pltpu.SemaphoreType.DMA((11,)),
        ],
        compiler_params=pltpu.CompilerParams(
            collective_id=0, has_side_effects=True, vmem_limit_bytes=48 * 1024 * 1024
        ),
    )(fields)
    return out[None]


def solution(mesh):
    return jax.shard_map(
        body,
        mesh=mesh,
        in_specs=(P("cuts", None, "gx", "gy", None),),
        out_specs=P("cuts", None, "gx", "gy", None),
        check_vma=False,
    )
```

profile of v0, /device:TPU:30, one launch (start us, length us, event | category | flops | bytes accessed | tf_op | source)
XLA Modules:
  0.0 68.8 jit_solution(13994635258281655535)
XLA Ops:
  0.0 0.0 copy-start
  0.0 1.7 %copy-done = f32[1,5,32,32,128]{4,3,2,1,0:T(8,128)S(1)} copy-done((f32[1,5,32,32,128]{4,3,2,1,0:T(8,128)S(1)}, f32[1,5,32,32,128]{4,3,2,1,0:T(8,128)}, u32[]{:S(2)}) %copy-start) | copy-done | bytes 2621464
  1.7 65.6 %shard_map.17 = f32[5,32,32,128]{3,2,1,0:T(8,128)S(1)} custom-call(f32[5,32,32,128]{3,2,1,0:T(8,128)S(1)} %bitcast.3), custom_call_target="tpu_custom_call" | custom-call | tf_op jit(solution)/shard_map/pallas_call | solution.py:339
  67.3 1.5 %copy.3 = f32[1,5,32,32,128]{4,3,2,1,0:T(8,128)} copy(f32[1,5,32,32,128]{4,3,2,1,0:T(8,128)S(1)} %bitcast.2) | data formatting | bytes 5242880
Async XLA Ops:
  0.0 1.7 %copy-start = (f32[1,5,32,32,128]{4,3,2,1,0:T(8,128)S(1)}, f32[1,5,32,32,128]{4,3,2,1,0:T(8,128)}, u32[]{:S(2)}) copy-start(f32[1,5,32,32,128]{4,3,2,1,0:T(8,128)} %param.1) | copy-start | bytes 7864324
where the time goes:
time: 68.9 us; the launch traced here: 68.8 us
  Pallas kernels  65.6 us (95%)
  local copies, waits for them, and re-layouts  3.23 us (5%)
    pallas_call x1, Pallas kernels, body(): pl.pallas_call(kernel, out_shape=jax.ShapeDtypeStruct(fields.shape, f32),...  65.6 us
    unnamed x3, local copies, waits for them, and re-layouts  3.23 us

commit v1 on v0

--- a/solution.py
+++ b/solution.py
@@ -101,7 +101,7 @@
 
 
 def kernel(x_ref, o_ref, s0, s1, fine, rs, hs, gr, cin, hin, cout,
-           load_sem, out_sem, halo_send, halo_recv, chain_send, chain_recv):
+           load_sem, halo_send, halo_recv, chain_send, chain_recv):
     n = lax.axis_index("cuts")
     gx = lax.axis_index("gx")
     gy = lax.axis_index("gy")
@@ -279,26 +279,34 @@
     def _(side):
         put_gr(side * 15)
 
-    def write_planes(j):
-        for y in (2 * j, 2 * j + 1):
-            pltpu.make_async_copy(fine.at[:, y], o_ref.at[:, :, y, :], out_sem).start()
-
     @pl.when(n == 0)
     def _():
-        pl.loop(0, NC)(write_planes)
+        @pl.loop(0, NB)
+        def _(y):
+            for f in FIELDS:
+                for x in range(0, NB, 8):
+                    o_ref[pl.ds(f * NB * NB + x * NB + y, 8, stride=NB), :] = fine[f, y, pl.ds(x, 8), :]
 
     def chain_row(j):
         out = coarse_of(cin, hin, j)
         for f in FIELDS:
             d = out[f] - gr[f, j]
+            gr[f, j] = d
             cout[f, j] = cout[f, j] + d
+
+    def result_row(j):
+        for f in FIELDS:
+            d = gr[f, j]
             low = jnp.where(even, d, lane_down(d))
             high = jnp.where(even, lane_up(d), d)
             for y in (2 * j, 2 * j + 1):
-                for start, part in ((0, low), (1, low), (16, high), (17, high)):
-                    span = pl.ds(start, 8, stride=2)
-                    fine[f, y, span, :] = fine[f, y, span, :] + part
-        write_planes(j)
+                for x, part in ((0, low), (1, low), (16, high), (17, high)):
+                    total = fine[f, y, pl.ds(x, 8, stride=2), :] + part
+                    o_ref[pl.ds(f * NB * NB + x * NB + y, 8, stride=2 * NB), :] = total
+
+    def start_next(late):
+        for k in (1, 2):
+            start_chain(k, late)
 
     for k in range(3):
         wait_chain(k, False)
@@ -307,8 +315,11 @@
     def _():
         pl.loop(n + 1, NC - 1 - n)(chain_row)
 
-    for k in (1, 2):
-        start_chain(k, False)
+    start_next(False)
+
+    @pl.when(n > 0)
+    def _():
+        pl.loop(n + 1, NC - 1 - n)(result_row)
 
     for k in range(3):
         wait_chain(k, True)
@@ -318,8 +329,12 @@
         pl.loop(0, n + 1)(chain_row)
         pl.loop(NC - 1 - n, NC)(chain_row)
 
-    for k in (1, 2):
-        start_chain(k, True)
+    start_next(True)
+
+    @pl.when(n > 0)
+    def _():
+        pl.loop(0, n + 1)(result_row)
+        pl.loop(NC - 1 - n, NC)(result_row)
 
     for copy in halos:
         copy.wait_send()
@@ -330,17 +345,15 @@
                 for copy in chain_copies(k, late):
                     copy.wait_send()
 
-    pltpu.make_async_copy(fine, o_ref, out_sem).wait()
-
 
 def body(slice_starts):
     fields = slice_starts[0]
     f32 = jnp.float32
     out = pl.pallas_call(
         kernel,
-        out_shape=jax.ShapeDtypeStruct(fields.shape, f32),
-        in_specs=[pl.BlockSpec(memory_space=pl.ANY)],
-        out_specs=pl.BlockSpec(memory_space=pl.ANY),
+        out_shape=pltpu.VMEM((5 * NB * NB, 128), f32),
+        in_specs=[pl.BlockSpec(memory_space=pltpu.HBM)],
+        out_specs=pl.BlockSpec(memory_space=pltpu.VMEM),
         scratch_shapes=[
             pltpu.VMEM((5, 36, 48, 128), f32),
             pltpu.VMEM((5, 34, 48, 128), f32),
@@ -352,17 +365,16 @@
             pltpu.VMEM((5, NC, 8, 128), f32),
             pltpu.VMEM((5, NC, 8, 128), f32),
             pltpu.SemaphoreType.DMA,
-            pltpu.SemaphoreType.DMA,
             pltpu.SemaphoreType.DMA((12,)),
             pltpu.SemaphoreType.DMA((12,)),
             pltpu.SemaphoreType.DMA((11,)),
             pltpu.SemaphoreType.DMA((11,)),
         ],
         compiler_params=pltpu.CompilerParams(
-            collective_id=0, has_side_effects=True, vmem_limit_bytes=48 * 1024 * 1024
+            collective_id=0, has_side_effects=True, vmem_limit_bytes=60 * 1024 * 1024
         ),
     )(fields)
-    return out[None]
+    return out.reshape((1,) + fields.shape)
 
 
 def solution(mesh):

time: 68.9 us -> 60.7 us (0.88)
  Pallas kernels: 65.6 us -> 59 us
  local copies, waits for them, and re-layouts: 3.23 us -> 1.49 us
    pallas_call x1, Pallas kernels: 65.6 us -> 59 us  [body(): pl.pallas_call(kernel, out_shape=pltpu.VMEM((5 * NB * NB, 128), f32), in_...]
    unnamed x3 -> x1, local copies, waits for them, and re-layouts: 3.23 us -> 1.49 us
where the time goes in v1:
time: 60.7 us; the launch traced here: 60.5 us
  Pallas kernels  59 us (97%)
  local copies, waits for them, and re-layouts  1.49 us (2%)
    pallas_call x1, Pallas kernels, body(): pl.pallas_call(kernel, out_shape=pltpu.VMEM((5 * NB * NB, 128), f32), in_...  59 us
    unnamed x1, local copies, waits for them, and re-layouts  1.49 us

profile of v1, /device:TPU:30, one launch (start us, length us, event | category | flops | bytes accessed | tf_op | source)
XLA Modules:
  0.0 60.5 jit_solution(2439978622442413033)
XLA Ops:
  0.0 59.0 %shard_map.17 = f32[5120,128]{1,0:T(8,128)S(1)} custom-call(f32[5,32,32,128]{3,2,1,0:T(8,128)} %bitcast.3), custom_call_target="tpu_custom_call" | custom-call | tf_op jit(solution)/shard_map/pallas_call | solution.py:352
  59.0 1.5 %copy.3 = f32[1,5,32,32,128]{4,3,2,1,0:T(8,128)} copy(f32[1,5,32,32,128]{4,3,2,1,0:T(8,128)S(1)} %bitcast.2) | data formatting | bytes 5242880

commit v2 on v1

v2 whole, which is shorter than its diff:
```python
import jax
import jax.numpy as jnp
from jax import lax
from jax.experimental import pallas as pl
from jax.experimental.pallas import tpu as pltpu
from jax.sharding import PartitionSpec as P

TIME_STEP = 0.1
VISCOSITY = 0.2
MESH = pl.DeviceIdType.MESH
NB = 32
NC = 16
X0 = 8
FIELDS = range(5)
HALO = 3
PARTS = ((1, 8), (9, 6))


def stencil(C, E, W, N, S, A, B, top, bottom, spacing, step):
    g = step / (2.0 * spacing)
    k = VISCOSITY * step / (spacing * spacing)
    centre = 1.0 - 6.0 * k
    zero = jnp.zeros_like(C[0])
    gu, gv, gw = g * C[0], g * C[1], g * C[2]
    ce, cw = k - gu, k + gu
    cn, cs = k - gv, k + gv
    ca = jnp.where(top, zero, k - gw)
    cb = jnp.where(bottom, zero, k + gw)
    out = []
    for q in range(4):
        out.append(
            (centre * C[q] + ce * E[q] + cw * W[q])
            + (cn * N[q] + cs * S[q])
            + (ca * A[q] + cb * B[q])
        )
    rise_p = jnp.where(top, zero, A[4]) - jnp.where(bottom, zero, B[4])
    rise_w = jnp.where(top, zero, A[2]) - jnp.where(bottom, zero, B[2])
    out[0] = out[0] - g * (E[4] - W[4])
    out[1] = out[1] - g * (N[4] - S[4])
    out[2] = out[2] + (step * C[3] - g * rise_p)
    out[3] = out[3] + step * C[2]
    out.append(C[4] - g * ((E[0] - W[0]) + (N[1] - S[1]) + rise_w))
    return out


def lanes():
    return lax.broadcasted_iota(jnp.int32, (8, 128), 1)


def sublanes():
    return lax.broadcasted_iota(jnp.int32, (8, 128), 0)


def lane_up(v, n=1):
    return pltpu.roll(v, 128 - n, v.ndim - 1)


def lane_down(v, n=1):
    return pltpu.roll(v, n, v.ndim - 1)


def fine_tile(src, dst, ys, yd, rs, rd, top, bottom):
    C = [src[f, ys, pl.ds(rs, 8), :] for f in FIELDS]
    E = [src[f, ys, pl.ds(rs + 1, 8), :] for f in FIELDS]
    W = [src[f, ys, pl.ds(rs - 1, 8), :] for f in FIELDS]
    N = [src[f, ys + 1, pl.ds(rs, 8), :] for f in FIELDS]
    S = [src[f, ys - 1, pl.ds(rs, 8), :] for f in FIELDS]
    A = [lane_up(c) for c in C]
    B = [lane_down(c) for c in C]
    out = stencil(C, E, W, N, S, A, B, top, bottom, 1.0, TIME_STEP)
    for f in FIELDS:
        dst[f, yd, pl.ds(rd, 8), :] = out[f]


def restrict_row(src, y, x0, even):
    out = []
    for f in FIELDS:
        halves = []
        for base in (x0, x0 + 16):
            total = None
            for plane in (y, y + 1):
                for start in (base, base + 1):
                    part = src[f, plane, pl.ds(start, 8, stride=2), :]
                    total = part if total is None else total + part
            halves.append(total)
        low, high = halves
        out.append(0.125 * jnp.where(even, low + lane_up(low), high + lane_down(high)))
    return out


def coarse_row(C, N, S, H, even, sub, top, bottom):
    E, W = [], []
    for f in FIELDS:
        r_w = pltpu.roll(C[f], 1, 0)
        r_e = pltpu.roll(C[f], 7, 0)
        mixed = jnp.where(sub == 0, jnp.where(even, r_w, H[f]), jnp.where(even, H[f], r_e))
        swapped = jnp.where(even, lane_up(mixed), lane_down(mixed))
        W.append(jnp.where(sub == 0, swapped, r_w))
        E.append(jnp.where(sub == 7, swapped, r_e))
    A = [lane_up(c, 2) for c in C]
    B = [lane_down(c, 2) for c in C]
    return stencil(C, E, W, N, S, A, B, top, bottom, 2.0, 2.0 * TIME_STEP)


def strip_rows(state, y, count, start, top, bottom):
    rows = pl.ds(y + HALO, count)
    here, east, west = (pl.ds(start + shift, 8) for shift in (0, 1, -1))
    C = [state[f, rows, here, :] for f in FIELDS]
    E = [state[f, rows, east, :] for f in FIELDS]
    W = [state[f, rows, west, :] for f in FIELDS]
    N = [state[f, pl.ds(y + HALO + 1, count), here, :] for f in FIELDS]
    S = [state[f, pl.ds(y + HALO - 1, count), here, :] for f in FIELDS]
    A = [lane_up(c, 2) for c in C]
    B = [lane_down(c, 2) for c in C]
    return stencil(C, E, W, N, S, A, B, top, bottom, 2.0, 2.0 * TIME_STEP)


def kernel(x_ref, o_ref, s0, s1, fine, rs, hs, gr, cout, chain0, chain1, chain2, rim0, rim1, rim2,
           packed0, packed1, packed2, edge0, edge1, edge2, late_own, late_rim, load_sem, halo_send, halo_recv, chain_send, chain_recv, pass_send, pass_recv):
    n = lax.axis_index("cuts")
    gx = lax.axis_index("gx")
    gy = lax.axis_index("gy")
    chain, rim = (chain0, chain1, chain2), (rim0, rim1, rim2)
    packed, edge = (packed0, packed1, packed2), (edge0, edge1, edge2)

    def at(dn, dx, dy):
        return (lax.rem(n + 4 + dn, 4), lax.rem(gx + 8 + dx, 8), lax.rem(gy + 8 + dy, 8))

    def remote(src, dst, where, send_sem, recv_sem):
        return pltpu.make_async_remote_copy(
            src_ref=src, dst_ref=dst, send_sem=send_sem, recv_sem=recv_sem,
            device_id=at(*where), device_id_type=MESH,
        )

    partners = [(0, dx, dy) for dx in (0, 1, -1) for dy in (1, -1, 0) if (dx, dy) != (0, 0)]
    partners += [(dn, 0, dy) for dn in (1, 2, 3) for dy in (1, -1, 0)]
    barrier = pltpu.get_barrier_semaphore()
    for p in partners:
        pl.semaphore_signal(barrier, inc=1, device_id=at(*p), device_id_type=MESH)

    @pl.loop(0, NB)
    def _(y):
        pltpu.make_async_copy(
            x_ref.at[:, :, y, :], s0.at[:, y + 2, pl.ds(X0, NB), :], load_sem
        ).start()

    pl.semaphore_wait(barrier, len(partners))

    halos = []

    def send(src, dst, dx, dy):
        i = len(halos)
        copy = remote(src, dst, (0, dx, dy), halo_send.at[i], halo_recv.at[i])
        copy.start()
        halos.append(copy)

    own, rows = pl.ds(2, NB), pl.ds(X0, NB)
    for step in range(2):
        send(x_ref.at[:, 30 + step, :, :], s0.at[:, own, 6 + step, :], 1, 0)
        send(x_ref.at[:, step, :, :], s0.at[:, own, 40 + step, :], -1, 0)
    for dx, x_from, x_to in ((1, 31, 7), (-1, 0, 40)):
        for dy, y_from, y_to in ((1, 31, 1), (-1, 0, 34)):
            send(x_ref.at[:, x_from, y_from, :], s0.at[:, y_to, x_to, :], dx, dy)

    lane, sub = lanes(), sublanes()
    even = lane % 2 == 0
    top, bottom = lane == 127, lane == 0
    ctop, cbottom = lane >= 126, lane <= 1

    def first_plane(y, starts):
        for r in starts:
            fine_tile(s0, s1, y + 2, y + 1, r, r, top, bottom)

    def second_plane(y, starts):
        for r in starts:
            fine_tile(s1, fine, y + 1, y, r + X0, r, top, bottom)

    def put_rs(j):
        out = restrict_row(s0, 2 * j + 2, X0, even)
        for f in FIELDS:
            rs[f, j + 1] = out[f]

    def put_hs(j):
        for f in FIELDS:
            total = None
            for plane in (2 * j + 2, 2 * j + 3):
                west = s0[f, plane, pl.ds(6, 8), :] + s0[f, plane, pl.ds(7, 8), :]
                east = s0[f, plane, pl.ds(33, 8), :] + s0[f, plane, pl.ds(34, 8), :]
                part = jnp.where(sub == 0, west, east)
                total = part if total is None else total + part
            hs[f, j] = 0.125 * (total + jnp.where(even, lane_up(total), lane_down(total)))

    def put_gr(j):
        C = [rs[f, j + 1] for f in FIELDS]
        N = [rs[f, j + 2] for f in FIELDS]
        S = [rs[f, j] for f in FIELDS]
        H = [hs[f, j] for f in FIELDS]
        out = coarse_row(C, N, S, H, even, sub, ctop, cbottom)
        for f in FIELDS:
            gr[f, j] = out[f]

    def put_e(j):
        out = restrict_row(fine, 2 * j, 0, even)
        for f in FIELDS:
            cout[f, lax.rem(j + 1, NC)] = out[f] - gr[f, j]

    def pairs(low, high, *jobs):
        @pl.loop(low, high, step=2)
        def _(j):
            for job in jobs:
                job(j)
                job(j + 1)

    pltpu.make_async_copy(x_ref, s0.at[:, own, rows, :], load_sem).wait()
    pairs(1, NB - 1, lambda y: first_plane(y, (15, 23, 31)))
    for copy in halos[:4]:
        copy.wait_send()
    for step in range(2):
        send(x_ref.at[:, :, 30 + step, :], s0.at[:, step, rows, :], 0, 1)
        send(x_ref.at[:, :, step, :], s0.at[:, 34 + step, rows, :], 0, -1)
    pairs(2, NB - 2, lambda y: second_plane(y, (8, 16)))

    @pl.when(n == 0)
    def _():
        gr[...] = jnp.zeros_like(gr)

    @pl.when(n > 0)
    def _():
        pairs(0, NC, put_rs)

    for copy in halos[:4]:
        copy.wait_recv()
    cols = pl.ds(8, 8)
    below, above = HALO - 1, HALO + NC

    def own_copies(k, m, part):
        def copy(src, dst, dy, i):
            return remote(src, dst, (m - k, 0, dy), chain_send.at[m - k - 1, i], chain_recv.at[k, i])

        if part == 3:
            return [
                copy(cout.at[:, pl.ds(0, 2)], late_own.at[k], 0, 1),
                copy(cout.at[:, 0], chain[k].at[:, below, cols, :], 1, 2),
                copy(cout.at[:, 1], chain[k].at[:, above, cols, :], -1, 3),
            ]
        if part == 2:
            if (k, m) != (1, 3):
                return []
            return [
                copy(cout.at[:, 15], chain[k].at[:, below - 1, cols, :], 1, 4),
                copy(cout.at[:, 2], chain[k].at[:, above + 1, cols, :], -1, 5),
            ]
        first, count = PARTS[part]
        dst = chain[k].at[:, pl.ds(HALO + first, count), cols, :]
        return [copy(cout.at[:, pl.ds(first + 1, count)], dst, 0, (0, 6)[part])]

    def start_own(part):
        for k in (0, 1, 2):
            if part == 2 and k != 1:
                continue

            @pl.when(n == k)
            def _():
                for m in (3, 2, 1):
                    if m > k:
                        for copy in own_copies(k, m, part):
                            copy.start()

    def pass_copies(k, m, part):
        copies = []
        wide = m - k

        def add(src, dst, dx, dy):
            i = len(copies) + 6 * part
            copies.append(remote(src, dst, (0, dx, dy), pass_send.at[k, i], pass_recv.at[k, i]))

        low, high = pl.ds(0, wide), pl.ds(8 - wide, wide)
        if part == 2:
            both = pl.ds(0, 2)
            if wide > 1:
                few, last = pl.ds(0, wide - 1), pl.ds(9 - wide, wide - 1)
                add(late_own.at[k, :, 0, last, :], rim[k].at[:, 0, last, :], 1, 1)
                add(late_own.at[k, :, 0, few, :], rim[k].at[:, 0, few, :], -1, 1)
                add(late_own.at[k, :, 1, last, :], rim[k].at[:, 1, last, :], 1, -1)
                add(late_own.at[k, :, 1, few, :], rim[k].at[:, 1, few, :], -1, -1)
            add(late_own.at[k, :, both, high, :], late_rim.at[k, :, both, high, :], 1, 0)
            add(late_own.at[k, :, both, low, :], late_rim.at[k, :, both, low, :], -1, 0)
            return copies
        span = (pl.ds(0, 4), pl.ds(4, 3))[part]
        add(packed[k].at[:, span, high, :], edge[k].at[:, span, high, :], 1, 0)
        add(packed[k].at[:, span, low, :], edge[k].at[:, span, low, :], -1, 0)
        if wide > 1 and (k, m) != (1, 3):
            deep = wide - 1
            src, dst, dy = ((HALO + 1, above + 1, -1), (above - 1 - deep, below - deep, 1))[part]
            add(chain[k].at[:, pl.ds(src, deep), cols, :], chain[k].at[:, pl.ds(dst, deep), cols, :], 0, dy)
        if wide > 2:
            src, dst, dy = ((HALO + 1, 3, -1), (above - 2, 2, 1))[part]
            add(chain[k].at[:, src, pl.ds(15, 1), :], rim[k].at[:, dst, pl.ds(7, 1), :], 1, dy)
            add(chain[k].at[:, src, pl.ds(8, 1), :], rim[k].at[:, dst, pl.ds(0, 1), :], -1, dy)
        return copies

    def pack(k, part):
        first, count = PARTS[part]
        half = count // 2
        one = chain[k][:, pl.ds(HALO + first, half), cols, :]
        two = chain[k][:, pl.ds(HALO + first + half, half), cols, :]
        upper = jnp.where(even, lane_up(two), one)
        lower = jnp.where(even, one, lane_down(two))
        packed[k][:, pl.ds(4 * part, half)] = jnp.where(sub < 4, lower, upper)

    def hand_on(m, part):
        for k in range(m):
            own_copies(k, m, part)[0].wait_recv()
            pack(k, part)
            for copy in pass_copies(k, m, part):
                copy.start()

    def outer_part(part):
        first, count = PARTS[part]
        pairs((1, 19)[part], (19, 31)[part], lambda y: first_plane(y, (7, 39)))
        pairs(2 * first, 2 * (first + count), lambda y: second_plane(y, (0, 24)))

        @pl.when(n > 0)
        def _():
            pairs(first, first + count, put_hs)
            pairs(first, first + count, put_gr)

        pairs(first, first + count, put_e)
        start_own(part)

    outer_part(0)
    outer_part(1)

    @pl.when(n > 0)
    def _():
        put_hs(0)
        put_hs(NC - 1)

    for m in (1, 2, 3):
        pl.when(n == m)(lambda: hand_on(m, 0))

    for copy in halos[4:]:
        copy.wait_recv()
    start_own(2)

    @pl.loop(0, 2)
    def _(side):
        first_plane(side * 33 - 1, (8, 16, 24, 32))
        first_plane(side * 31, (7, 15, 23, 31, 39))

    @pl.loop(0, 2)
    def _(side):
        second_plane(side * 30, (0, 8, 16, 24))
        second_plane(side * 30 + 1, (0, 8, 16, 24))

    @pl.when(n > 0)
    def _():
        put_rs(-1)
        put_rs(NC)
        put_gr(0)
        put_gr(NC - 1)

    put_e(0)
    put_e(NC - 1)
    start_own(3)

    @pl.when(n == 0)
    def _():
        @pl.loop(0, NB)
        def _(y):
            for f in FIELDS:
                for x in range(0, NB, 8):
                    o_ref[pl.ds(f * NB * NB + x * NB + y, 8, stride=NB), :] = fine[f, y, pl.ds(x, 8), :]

    def widen(k, rows, own_cols, west, east):
        chain[k][:, rows, pl.ds(0, 8), :] = jnp.where(even, west, lane_down(own_cols))
        chain[k][:, rows, pl.ds(16, 8), :] = jnp.where(even, lane_up(own_cols), east)

    def widen_row(k, row, beside):
        widen(k, row, chain[k][:, row, cols, :], lane_up(beside), lane_down(beside))

    def widen_part(k, part):
        first, count = PARTS[part]
        half = count // 2
        beside = edge[k][:, pl.ds(4 * part, half)]
        one, two = (pl.ds(HALO + first + start, half) for start in (0, half))
        widen(k, one, chain[k][:, one, cols, :], lane_up(beside), lane_down(beside))
        widen(k, two, chain[k][:, two, cols, :], beside, beside)

    def level_rows(k, y, count):
        at_rows = pl.ds(y + HALO, count)
        out = [strip_rows(chain[k - 1], y, count, start, ctop, cbottom) for start in (4, 12)]
        for start, part in zip((4, 12), out):
            for f in FIELDS:
                here = (f, at_rows, pl.ds(start, 8), slice(None))
                chain[k][here] = chain[k][here] + part[f]

    def result_rows(m, y, count):
        out = strip_rows(chain[m - 1], y, count, 8, ctop, cbottom)
        for f in FIELDS:
            d = out[f] - gr[f, pl.ds(y, count)]
            low = jnp.where(even, d, lane_down(d))
            high = jnp.where(even, lane_up(d), d)
            for i in range(count):
                for half in range(2):
                    plane = 2 * (y + i) + half
                    for x, part in ((0, low), (1, low), (16, high), (17, high)):
                        total = fine[f, plane, pl.ds(x, 8, stride=2), :] + part[i]
                        o_ref[pl.ds(f * NB * NB + x * NB + plane, 8, stride=2 * NB), :] = total

    def finish(m):
        passes = [[pass_copies(k, m, part) for part in range(3)] for k in range(m)]
        hand_on(m, 1)
        for k in range(m):
            own_copies(k, m, 3)[0].wait_recv()
            for copy in passes[k][2]:
                copy.start()
        for k in range(m):
            for part in (0, 1):
                for copy in passes[k][part]:
                    copy.wait()
                widen_part(k, part)
            if m - k > 2:
                widen_row(k, HALO - 2, rim[k][:, 2])
                widen_row(k, HALO + NC + 1, rim[k][:, 3])
        for k in range(1, m):
            pl.loop(k + 1, NC - 1 - k, step=2)(lambda y: level_rows(k, y, 2))
        pl.loop(m + 1, NC - 1 - m, step=2)(lambda y: result_rows(m, y, 2))
        for k in range(m):
            for copy in passes[k][2]:
                copy.wait()
            for copy in own_copies(k, m, 2) + own_copies(k, m, 3)[1:]:
                copy.wait_recv()
            for i, row in ((0, HALO + NC - 1), (1, HALO)):
                own_cols = late_own[k, :, i]
                chain[k][:, row, cols, :] = own_cols
                beside = late_rim[k, :, i]
                widen(k, row, own_cols, lane_up(beside), lane_down(beside))
            if m - k > 1:
                widen_row(k, below, rim[k][:, 0])
                widen_row(k, above, rim[k][:, 1])
        for k in range(1, m):
            level_rows(k, k - m, m + 1)
            level_rows(k, NC - 1 - k, m + 1)
        result_rows(m, 0, m + 1)
        result_rows(m, NC - 1 - m, m + 1)

    for m in (1, 2, 3):
        pl.when(n == m)(lambda: finish(m))

    for copy in halos[4:]:
        copy.wait_send()
    for k in (0, 1, 2):
        @pl.when(n == k)
        def _():
            for m in range(k + 1, 4):
                for part in range(4):
                    for copy in own_copies(k, m, part):
                        copy.wait_send()


def body(slice_starts):
    fields = slice_starts[0]
    f32 = jnp.float32
    out = pl.pallas_call(
        kernel,
        out_shape=pltpu.VMEM((5 * NB * NB, 128), f32),
        in_specs=[pl.BlockSpec(memory_space=pltpu.HBM)],
        out_specs=pl.BlockSpec(memory_space=pltpu.VMEM),
        scratch_shapes=[
            pltpu.VMEM((5, 36, 48, 128), f32),
            pltpu.VMEM((5, 34, 48, 128), f32),
            pltpu.VMEM((5, NB, NB, 128), f32),
            pltpu.VMEM((5, NC + 2, 8, 128), f32),
            pltpu.VMEM((5, NC, 8, 128), f32),
            pltpu.VMEM((5, NC, 8, 128), f32),
            pltpu.VMEM((5, NC, 8, 128), f32),
            *[pltpu.VMEM((5, NC + 2 * HALO, 24, 128), f32) for _ in range(3)],
            *[pltpu.VMEM((5, 4, 8, 128), f32) for _ in range(3)],
            *[pltpu.VMEM((5, 7, 8, 128), f32) for _ in range(3)],
            *[pltpu.VMEM((5, 7, 8, 128), f32) for _ in range(3)],
            pltpu.VMEM((3, 5, 2, 8, 128), f32),
            pltpu.VMEM((3, 5, 2, 8, 128), f32),
            pltpu.SemaphoreType.DMA,
            pltpu.SemaphoreType.DMA((12,)),
            pltpu.SemaphoreType.DMA((12,)),
            pltpu.SemaphoreType.DMA((3, 7)),
            pltpu.SemaphoreType.DMA((3, 7)),
            pltpu.SemaphoreType.DMA((3, 18)),
            pltpu.SemaphoreType.DMA((3, 18)),
        ],
        compiler_params=pltpu.CompilerParams(
            collective_id=0, has_side_effects=True, vmem_limit_bytes=60 * 1024 * 1024
        ),
    )(fields)
    return out.reshape((1,) + fields.shape)


def solution(mesh):
    return jax.shard_map(
        body,
        mesh=mesh,
        in_specs=(P("cuts", None, "gx", "gy", None),),
        out_specs=P("cuts", None, "gx", "gy", None),
        check_vma=False,
    )
```

time: 60.7 us -> 52 us (0.86)
  the two profiles are of different devices: /device:TPU:30 before, /device:TPU:7 now
where the time goes in v2:
time: 52 us; the launch traced here: 51.9 us
  Pallas kernels  50.4 us (97%)
  local copies, waits for them, and re-layouts  1.49 us (3%)
    pallas_call x1, Pallas kernels, body(): pl.pallas_call(kernel, out_shape=pltpu.VMEM((5 * NB * NB, 128), f32), in_...  50.4 us
    unnamed x1, local copies, waits for them, and re-layouts  1.49 us

profile of v2, /device:TPU:7, one launch (start us, length us, event | category | flops | bytes accessed | tf_op | source)
XLA Modules:
  0.0 51.9 jit_solution(17278603182499154741)
XLA Ops:
  0.0 50.4 %shard_map.17 = f32[5120,128]{1,0:T(8,128)S(1)} custom-call(f32[5,32,32,128]{3,2,1,0:T(8,128)} %bitcast.3), custom_call_target="tpu_custom_call" | custom-call | tf_op jit(solution)/shard_map/pallas_call | solution.py:465
  50.4 1.5 %copy.3 = f32[1,5,32,32,128]{4,3,2,1,0:T(8,128)} copy(f32[1,5,32,32,128]{4,3,2,1,0:T(8,128)S(1)} %bitcast.2) | data formatting | bytes 5242880

commit v3 on v2

--- a/solution.py
+++ b/solution.py
@@ -13,6 +13,7 @@
 X0 = 8
 FIELDS = range(5)
 HALO = 3
+RELAYED = {(1, 3): 2, (0, 2): 3}
 PARTS = ((1, 8), (9, 6))
 
 
@@ -116,7 +117,7 @@
 
 
 def kernel(x_ref, o_ref, s0, s1, fine, rs, hs, gr, cout, chain0, chain1, chain2, rim0, rim1, rim2,
-           packed0, packed1, packed2, edge0, edge1, edge2, late_own, late_rim, load_sem, halo_send, halo_recv, chain_send, chain_recv, pass_send, pass_recv):
+           packed0, packed1, packed2, edge0, edge1, edge2, late_own, late_rim, load_sem, halo_send, halo_recv, chain_send, chain_recv, pass_send, pass_recv, ready):
     n = lax.axis_index("cuts")
     gx = lax.axis_index("gx")
     gy = lax.axis_index("gy")
@@ -133,7 +134,7 @@
         )
 
     partners = [(0, dx, dy) for dx in (0, 1, -1) for dy in (1, -1, 0) if (dx, dy) != (0, 0)]
-    partners += [(dn, 0, dy) for dn in (1, 2, 3) for dy in (1, -1, 0)]
+    partners += [(dn, 0, 0) for dn in (1, 2, 3)]
     barrier = pltpu.get_barrier_semaphore()
     for p in partners:
         pl.semaphore_signal(barrier, inc=1, device_id=at(*p), device_id_type=MESH)
@@ -145,6 +146,8 @@
         ).start()
 
     pl.semaphore_wait(barrier, len(partners))
+    for dn in (1, 2, 3):
+        pl.semaphore_signal(ready, inc=1, device_id=at(dn, 0, 0), device_id_type=MESH)
 
     halos = []
 
@@ -161,6 +164,10 @@
     for dx, x_from, x_to in ((1, 31, 7), (-1, 0, 40)):
         for dy, y_from, y_to in ((1, 31, 1), (-1, 0, 34)):
             send(x_ref.at[:, x_from, y_from, :], s0.at[:, y_to, x_to, :], dx, dy)
+
+    for step in range(2):
+        send(x_ref.at[:, :, 30 + step, :], s0.at[:, step, rows, :], 0, 1)
+        send(x_ref.at[:, :, step, :], s0.at[:, 34 + step, rows, :], 0, -1)
 
     lane, sub = lanes(), sublanes()
     even = lane % 2 == 0
@@ -213,11 +220,6 @@
 
     pltpu.make_async_copy(x_ref, s0.at[:, own, rows, :], load_sem).wait()
     pairs(1, NB - 1, lambda y: first_plane(y, (15, 23, 31)))
-    for copy in halos[:4]:
-        copy.wait_send()
-    for step in range(2):
-        send(x_ref.at[:, :, 30 + step, :], s0.at[:, step, rows, :], 0, 1)
-        send(x_ref.at[:, :, step, :], s0.at[:, 34 + step, rows, :], 0, -1)
     pairs(2, NB - 2, lambda y: second_plane(y, (8, 16)))
 
     @pl.when(n == 0)
@@ -238,11 +240,21 @@
             return remote(src, dst, (m - k, 0, dy), chain_send.at[m - k - 1, i], chain_recv.at[k, i])
 
         if part == 3:
-            return [
+            copies = [
                 copy(cout.at[:, pl.ds(0, 2)], late_own.at[k], 0, 1),
                 copy(cout.at[:, 0], chain[k].at[:, below, cols, :], 1, 2),
                 copy(cout.at[:, 1], chain[k].at[:, above, cols, :], -1, 3),
             ]
+            few = m - k - 1
+            if few:
+                for row, dy in ((0, 1), (1, -1)):
+                    for span, dx in ((pl.ds(8 - few, few), 1), (pl.ds(0, few), -1)):
+                        i = len(copies) + 4
+                        copies.append(remote(
+                            cout.at[:, row, span, :], rim[k].at[:, row, span, :], (m - k, dx, dy),
+                            chain_send.at[m - k - 1, i], chain_recv.at[k, i],
+                        ))
+            return copies
         if part == 2:
             if (k, m) != (1, 3):
                 return []
@@ -252,7 +264,11 @@
             ]
         first, count = PARTS[part]
         dst = chain[k].at[:, pl.ds(HALO + first, count), cols, :]
-        return [copy(cout.at[:, pl.ds(first + 1, count)], dst, 0, (0, 6)[part])]
+        i = (0, 6)[part]
+        if (k, m) in RELAYED:
+            dn = m - RELAYED[k, m]
+            return [remote(dst, dst, (dn, 0, 0), chain_send.at[m - k - 1, i], chain_recv.at[k, i])]
+        return [copy(cout.at[:, pl.ds(first + 1, count)], dst, 0, i)]
 
     def start_own(part):
         for k in (0, 1, 2):
@@ -262,7 +278,7 @@
             @pl.when(n == k)
             def _():
                 for m in (3, 2, 1):
-                    if m > k:
+                    if m > k and not (part < 2 and (k, m) in RELAYED):
                         for copy in own_copies(k, m, part):
                             copy.start()
 
@@ -277,12 +293,6 @@
         low, high = pl.ds(0, wide), pl.ds(8 - wide, wide)
         if part == 2:
             both = pl.ds(0, 2)
-            if wide > 1:
-                few, last = pl.ds(0, wide - 1), pl.ds(9 - wide, wide - 1)
-                add(late_own.at[k, :, 0, last, :], rim[k].at[:, 0, last, :], 1, 1)
-                add(late_own.at[k, :, 0, few, :], rim[k].at[:, 0, few, :], -1, 1)
-                add(late_own.at[k, :, 1, last, :], rim[k].at[:, 1, last, :], 1, -1)
-                add(late_own.at[k, :, 1, few, :], rim[k].at[:, 1, few, :], -1, -1)
             add(late_own.at[k, :, both, high, :], late_rim.at[k, :, both, high, :], 1, 0)
             add(late_own.at[k, :, both, low, :], late_rim.at[k, :, both, low, :], -1, 0)
             return copies
@@ -309,8 +319,11 @@
         packed[k][:, pl.ds(4 * part, half)] = jnp.where(sub < 4, lower, upper)
 
     def hand_on(m, part):
-        for k in range(m):
+        for k in ((), (0,), (1, 0), (0, 2, 1))[m]:
             own_copies(k, m, part)[0].wait_recv()
+            for (first, last), via in RELAYED.items():
+                if (first, via) == (k, m):
+                    own_copies(first, last, part)[0].start()
             pack(k, part)
             for copy in pass_copies(k, m, part):
                 copy.start()
@@ -336,11 +349,15 @@
         put_hs(0)
         put_hs(NC - 1)
 
-    for m in (1, 2, 3):
-        pl.when(n == m)(lambda: hand_on(m, 0))
+    for m, parts in ((1, (0, 1)), (2, (0,)), (3, (0, 1))):
+        @pl.when(n == m)
+        def _():
+            for part in parts:
+                hand_on(m, part)
 
     for copy in halos[4:]:
         copy.wait_recv()
+    pl.semaphore_wait(ready, 3)
     start_own(2)
 
     @pl.loop(0, 2)
@@ -387,12 +404,12 @@
         widen(k, one, chain[k][:, one, cols, :], lane_up(beside), lane_down(beside))
         widen(k, two, chain[k][:, two, cols, :], beside, beside)
 
-    def level_rows(k, y, count):
-        at_rows = pl.ds(y + HALO, count)
-        out = [strip_rows(chain[k - 1], y, count, start, ctop, cbottom) for start in (4, 12)]
-        for start, part in zip((4, 12), out):
+    def level_rows(k, count, *firsts):
+        blocks = [(y, start) for y in firsts for start in (4, 12)]
+        out = [strip_rows(chain[k - 1], y, count, start, ctop, cbottom) for y, start in blocks]
+        for (y, start), part in zip(blocks, out):
             for f in FIELDS:
-                here = (f, at_rows, pl.ds(start, 8), slice(None))
+                here = (f, pl.ds(y + HALO, count), pl.ds(start, 8), slice(None))
                 chain[k][here] = chain[k][here] + part[f]
 
     def result_rows(m, y, count):
@@ -410,7 +427,8 @@
 
     def finish(m):
         passes = [[pass_copies(k, m, part) for part in range(3)] for k in range(m)]
-        hand_on(m, 1)
+        if m == 2:
+            hand_on(m, 1)
         for k in range(m):
             own_copies(k, m, 3)[0].wait_recv()
             for copy in passes[k][2]:
@@ -423,8 +441,11 @@
             if m - k > 2:
                 widen_row(k, HALO - 2, rim[k][:, 2])
                 widen_row(k, HALO + NC + 1, rim[k][:, 3])
+        if m == 2:
+            for part in (0, 1):
+                own_copies(1, 3, part)[0].wait_send()
         for k in range(1, m):
-            pl.loop(k + 1, NC - 1 - k, step=2)(lambda y: level_rows(k, y, 2))
+            pl.loop(k + 1, NC - 1 - k, step=2)(lambda y: level_rows(k, 2, y))
         pl.loop(m + 1, NC - 1 - m, step=2)(lambda y: result_rows(m, y, 2))
         for k in range(m):
             for copy in passes[k][2]:
@@ -440,23 +461,28 @@
                 widen_row(k, below, rim[k][:, 0])
                 widen_row(k, above, rim[k][:, 1])
         for k in range(1, m):
-            level_rows(k, k - m, m + 1)
-            level_rows(k, NC - 1 - k, m + 1)
+            level_rows(k, m + 1, k - m, NC - 1 - k)
         result_rows(m, 0, m + 1)
         result_rows(m, NC - 1 - m, m + 1)
 
     for m in (1, 2, 3):
         pl.when(n == m)(lambda: finish(m))
 
-    for copy in halos[4:]:
+    for copy in halos:
         copy.wait_send()
     for k in (0, 1, 2):
         @pl.when(n == k)
         def _():
             for m in range(k + 1, 4):
                 for part in range(4):
-                    for copy in own_copies(k, m, part):
-                        copy.wait_send()
+                    if not (part < 2 and (k, m) in RELAYED):
+                        for copy in own_copies(k, m, part):
+                            copy.wait_send()
+
+    @pl.when(n == 3)
+    def _():
+        for part in (0, 1):
+            own_copies(0, 2, part)[0].wait_send()
 
 
 def body(slice_starts):
@@ -484,10 +510,11 @@
             pltpu.SemaphoreType.DMA,
             pltpu.SemaphoreType.DMA((12,)),
             pltpu.SemaphoreType.DMA((12,)),
-            pltpu.SemaphoreType.DMA((3, 7)),
-            pltpu.SemaphoreType.DMA((3, 7)),
-            pltpu.SemaphoreType.DMA((3, 18)),
-            pltpu.SemaphoreType.DMA((3, 18)),
+            pltpu.SemaphoreType.DMA((3, 11)),
+            pltpu.SemaphoreType.DMA((3, 11)),
+            pltpu.SemaphoreType.DMA((3, 14)),
+            pltpu.SemaphoreType.DMA((3, 14)),
+            pltpu.SemaphoreType.REGULAR,
         ],
         compiler_params=pltpu.CompilerParams(
             collective_id=0, has_side_effects=True, vmem_limit_bytes=60 * 1024 * 1024

time: 52 us -> 48.8 us (0.938)
  Pallas kernels: 50.4 us -> 46.8 us
    pallas_call x1, Pallas kernels: 50.4 us -> 46.8 us  [body(): pl.pallas_call(kernel, out_shape=pltpu.VMEM((5 * NB * NB, 128), f32), in_...]
where the time goes in v3:
time: 48.8 us; the launch traced here: 48.3 us
  Pallas kernels  46.8 us (96%)
  local copies, waits for them, and re-layouts  1.49 us (3%)
    pallas_call x1, Pallas kernels, body(): pl.pallas_call(kernel, out_shape=pltpu.VMEM((5 * NB * NB, 128), f32), in_...  46.8 us
    unnamed x1, local copies, waits for them, and re-layouts  1.49 us

profile of v3, /device:TPU:7, one launch (start us, length us, event | category | flops | bytes accessed | tf_op | source)
XLA Modules:
  0.0 48.3 jit_solution(11621845701348090210)
XLA Ops:
  0.0 46.8 %shard_map.17 = f32[5120,128]{1,0:T(8,128)S(1)} custom-call(f32[5,32,32,128]{3,2,1,0:T(8,128)} %bitcast.3), custom_call_target="tpu_custom_call" | custom-call | tf_op jit(solution)/shard_map/pallas_call | solution.py:491
  46.8 1.5 %copy.3 = f32[1,5,32,32,128]{4,3,2,1,0:T(8,128)} copy(f32[1,5,32,32,128]{4,3,2,1,0:T(8,128)S(1)} %bitcast.2) | data formatting | bytes 5242880

commit v4 on v3

--- a/solution.py
+++ b/solution.py
@@ -318,8 +318,8 @@
         lower = jnp.where(even, one, lane_down(two))
         packed[k][:, pl.ds(4 * part, half)] = jnp.where(sub < 4, lower, upper)
 
-    def hand_on(m, part):
-        for k in ((), (0,), (1, 0), (0, 2, 1))[m]:
+    def hand_on(m, part, sources):
+        for k in sources:
             own_copies(k, m, part)[0].wait_recv()
             for (first, last), via in RELAYED.items():
                 if (first, via) == (k, m):
@@ -349,26 +349,28 @@
         put_hs(0)
         put_hs(NC - 1)
 
-    for m, parts in ((1, (0, 1)), (2, (0,)), (3, (0, 1))):
+    arrivals = (
+        (1, ((0, (0,)), (1, (0,)))),
+        (2, ((0, (1,)), (1, (1,)), (0, (0,)))),
+        (3, ((0, (0, 2)), (1, (0,)), (0, (1,)), (1, (2, 1)))),
+    )
+    for m, order in arrivals:
         @pl.when(n == m)
         def _():
-            for part in parts:
-                hand_on(m, part)
+            for part, sources in order:
+                hand_on(m, part, sources)
 
     for copy in halos[4:]:
         copy.wait_recv()
     pl.semaphore_wait(ready, 3)
     start_own(2)
 
-    @pl.loop(0, 2)
-    def _(side):
-        first_plane(side * 33 - 1, (8, 16, 24, 32))
-        first_plane(side * 31, (7, 15, 23, 31, 39))
-
-    @pl.loop(0, 2)
-    def _(side):
-        second_plane(side * 30, (0, 8, 16, 24))
-        second_plane(side * 30 + 1, (0, 8, 16, 24))
+    for y in (-1, NB):
+        first_plane(y, (8, 16, 24, 32))
+    for y in (0, NB - 1):
+        first_plane(y, (7, 15, 23, 31, 39))
+    for y in (0, 1, NB - 2, NB - 1):
+        second_plane(y, (0, 8, 16, 24))
 
     @pl.when(n > 0)
     def _():
@@ -412,10 +414,10 @@
                 here = (f, pl.ds(y + HALO, count), pl.ds(start, 8), slice(None))
                 chain[k][here] = chain[k][here] + part[f]
 
-    def result_rows(m, y, count):
-        out = strip_rows(chain[m - 1], y, count, 8, ctop, cbottom)
-        for f in FIELDS:
-            d = out[f] - gr[f, pl.ds(y, count)]
+    def result_rows(m, count, *firsts):
+        out = [strip_rows(chain[m - 1], y, count, 8, ctop, cbottom) for y in firsts]
+        for (y, terms), f in [(block, f) for block in zip(firsts, out) for f in FIELDS]:
+            d = terms[f] - gr[f, pl.ds(y, count)]
             low = jnp.where(even, d, lane_down(d))
             high = jnp.where(even, lane_up(d), d)
             for i in range(count):
@@ -428,7 +430,7 @@
     def finish(m):
         passes = [[pass_copies(k, m, part) for part in range(3)] for k in range(m)]
         if m == 2:
-            hand_on(m, 1)
+            hand_on(m, 1, (0,))
         for k in range(m):
             own_copies(k, m, 3)[0].wait_recv()
             for copy in passes[k][2]:
@@ -446,7 +448,7 @@
                 own_copies(1, 3, part)[0].wait_send()
         for k in range(1, m):
             pl.loop(k + 1, NC - 1 - k, step=2)(lambda y: level_rows(k, 2, y))
-        pl.loop(m + 1, NC - 1 - m, step=2)(lambda y: result_rows(m, y, 2))
+        pl.loop(m + 1, NC - 1 - m, step=2)(lambda y: result_rows(m, 2, y))
         for k in range(m):
             for copy in passes[k][2]:
                 copy.wait()
@@ -462,8 +464,7 @@
                 widen_row(k, above, rim[k][:, 1])
         for k in range(1, m):
             level_rows(k, m + 1, k - m, NC - 1 - k)
-        result_rows(m, 0, m + 1)
-        result_rows(m, NC - 1 - m, m + 1)
+        result_rows(m, m + 1, 0, NC - 1 - m)
 
     for m in (1, 2, 3):
         pl.when(n == m)(lambda: finish(m))

time: 48.8 us -> 48.6 us (level)
  no operation moved by 1% of the time
where the time goes in v4:
time: 48.6 us; the launch traced here: 48.1 us
  Pallas kernels  46.6 us (96%)
  local copies, waits for them, and re-layouts  1.49 us (3%)
    pallas_call x1, Pallas kernels, body(): pl.pallas_call(kernel, out_shape=pltpu.VMEM((5 * NB * NB, 128), f32), in_...  46.6 us
    unnamed x1, local copies, waits for them, and re-layouts  1.49 us

profile of v4, /device:TPU:7, one launch (start us, length us, event | category | flops | bytes accessed | tf_op | source)
XLA Modules:
  0.0 48.1 jit_solution(3249366201203013107)
XLA Ops:
  0.0 46.6 %shard_map.17 = f32[5120,128]{1,0:T(8,128)S(1)} custom-call(f32[5,32,32,128]{3,2,1,0:T(8,128)} %bitcast.3), custom_call_target="tpu_custom_call" | custom-call | tf_op jit(solution)/shard_map/pallas_call | solution.py:492
  46.6 1.5 %copy.3 = f32[1,5,32,32,128]{4,3,2,1,0:T(8,128)} copy(f32[1,5,32,32,128]{4,3,2,1,0:T(8,128)S(1)} %bitcast.2) | data formatting | bytes 5242880
